TPU v7x, 32 devices: a whole 2x2x4 slice. The times are simulated.
32 devices in a mesh: cin: 8 (over z, x), cout: 2 (over y), depth: 2 (over core).
Axes of the slice: x: 2, y: 2, z: 4, core: 2. Of those that a mesh axis runs over, the one named last changes fastest.
Arguments:
- features: bfloat16 [8, 512, 4, 128], P(None, 'cin', 'depth'), may hold values from -6 to 6
- kernel: bfloat16 [27, 512, 512], P(None, 'cout', 'cin'), may hold values from -0.0546875 to 0.0546875
- grad_out: bfloat16 [8, 512, 4, 128], P('cin', 'cout', 'depth'), may hold values from -6 to 6
Outputs:
- output: bfloat16 [8, 512, 4, 128], P('cin', 'cout', 'depth')
- input_grad: bfloat16 [8, 512, 4, 128], P('cout', 'cin', 'depth')
- kernel_grad: float32 [27, 512, 512], P(None, 'cout', 'cin')
All inputs are finite; a program needn't handle non-finite values.
Results may differ from a plain program's by a relative error of at most 0.001.
Values may be sent and summed in bfloat16 or wider, within the bound.
No kernel may reach another device: no remote copies, remote signals or barrier semaphores. Data moves between devices by JAX's collectives and lax.ppermute only.
A program may use at most 128 MiB of HBM per device.

v0:
```python
import math
import jax
import jax.numpy as jnp
from jax import lax
from jax.sharding import PartitionSpec as P


def padded_2(x, sides, width):
    for axis, dim in sides:
        size, length = (lax.axis_size(axis), x.shape[dim])
        up = [(i, (i + 1) % size) for i in range(size - 1)]
        down = [(j, i) for i, j in up]
        last = lax.slice_in_dim(x, length - width, length, axis=dim)
        first = lax.slice_in_dim(x, 0, width, axis=dim)
        before = lax.ppermute(last, axis, up)
        after = lax.ppermute(first, axis, down)
        x = jnp.concatenate([before, x, after], axis=dim)
    return x


def conv_rows(padded, weight, count, slab, width):
    total = None
    for depth_off in range(3):
        pieces = [
            padded[
                row_off : row_off + count,
                :,
                depth_off : depth_off + slab,
                col_off : col_off + width,
            ]
            for row_off in range(3)
            for col_off in range(3)
        ]
        stacked = jnp.stack(pieces, axis=1)
        term = jnp.einsum(
            "toc,htcdw->hodw",
            weight[9 * depth_off : 9 * depth_off + 9],
            stacked,
            preferred_element_type=jnp.float32,
        )
        total = term if total is None else total + term
    return total


def weight_terms(padded, grad_own, count, slab, width):
    parts = []
    for depth_off in range(3):
        pieces = [
            padded[
                row_off : row_off + count,
                :,
                depth_off : depth_off + slab,
                col_off : col_off + width,
            ]
            for row_off in range(3)
            for col_off in range(3)
        ]
        stacked = jnp.stack(pieces, axis=1)
        parts.append(
            jnp.einsum("hodw,htcdw->toc", grad_own, stacked, preferred_element_type=jnp.float32)
        )
    return jnp.concatenate(parts, axis=0)


def per_device(features, kernel, grad_out):
    rows_all = features.shape[0]
    slab = features.shape[2]
    width = features.shape[3]
    chan_in = features.shape[1]
    rows_own = rows_all // lax.axis_size("cin")
    slab_ext = padded_2(features, (("depth", 2),), 1)
    feat_pad = jnp.pad(slab_ext, ((1, 1), (0, 0), (0, 0), (1, 1)))
    block = feat_pad
    output = lax.psum_scatter(
        conv_rows(block, kernel, lax.axis_size("cin") * rows_own, slab, width),
        "cin",
        scatter_dimension=0,
        tiled=True,
    ).astype(jnp.bfloat16)
    grad_full = lax.all_gather(grad_out, "cin", axis=0, tiled=True)
    grad_full = padded_2(grad_full, (("depth", 2),), 1)
    grad_pad = jnp.pad(grad_full, ((1, 1), (0, 0), (0, 0), (0, 0)))
    rows_grad = rows_all // lax.axis_size("cout")
    block = grad_pad
    total = jnp.zeros((lax.axis_size("cout") * rows_grad, chan_in, slab, width), jnp.float32)
    for depth_off in range(3):
        part = block[:, :, 2 - depth_off : 2 - depth_off + slab, :]
        mixed = jnp.einsum(
            "toc,hodw->thcdw",
            kernel[9 * depth_off : 9 * depth_off + 9],
            part,
            preferred_element_type=jnp.float32,
        )
        mixed = jnp.pad(mixed, ((0, 0), (0, 0), (0, 0), (0, 0), (1, 1)))
        for row_off in range(3):
            for col_off in range(3):
                total = (
                    total
                    + mixed[
                        3 * row_off + col_off,
                        2 - row_off : 2 - row_off + lax.axis_size("cout") * rows_grad,
                        :,
                        :,
                        2 - col_off : 2 - col_off + width,
                    ]
                )
    input_grad = lax.psum_scatter(total, "cout", scatter_dimension=0, tiled=True).astype(
        jnp.bfloat16
    )
    grad_own = grad_full[:, :, 1 : 1 + slab, :]
    local_terms = weight_terms(feat_pad, grad_own, rows_all, slab, width)
    summed = lax.psum(local_terms, "depth")
    cells = rows_all * slab * lax.axis_size("depth") * width
    kernel_grad = summed * (1.0 / math.sqrt(cells))
    return (output, input_grad, kernel_grad)


def solution(mesh):
    return jax.shard_map(
        per_device,
        mesh=mesh,
        in_specs=(
            P(None, "cin", "depth", None),
            P(None, "cout", "cin"),
            P("cin", "cout", "depth", None),
        ),
        out_specs=(
            P("cin", "cout", "depth", None),
            P("cout", "cin", "depth", None),
            P(None, "cout", "cin"),
        ),
        check_vma=False,
    )
```

profile of v0, /device:TPU:0, one launch (start us, length us, event | category | flops | bytes accessed | tf_op | source)
XLA Modules:
  0.0 189.4 jit_solution(8112478354780090528)
XLA Ops:
  7.2 1.0 copy.40
  8.2 2.4 %collective-permute-start = (bf16[8,64,1,128]{3,1,2,0:T(8,128)(2,1)S(1)}, bf16[8,64,1,128]{3,1,2,0:T(8,128)(2,1)S(1)}, u32[]{:S(2)}, u32[]{:S(2)}) collective-permute-start(bf16[8,64,1,128]{3,1,2,0:T(8,128)(2,1)S(1)} %get-tuple-element.25), channel_id=1, source_target_pairs={{0,1},{2,3},{4,5},{6,7},{8,9},{10,11},{12,13},{14,15},{16,17},{18,... | collective-permute-start | bytes 393224 | tf_op jit(solution)/shard_map/ppermute | solution.py:15
  10.6 1.3 collective-permute-start.1
  11.9 1.6 copy.55
  18.4 0.9 fusion.84
  19.3 1.0 fusion.83
  20.3 0.9 fusion.82
  22.8 0.9 fusion.81
  26.9 0.9 fusion.80
  27.8 0.9 fusion.79
  28.7 28.0 %all-gather.2.cloned.1.call-done = bf16[8,256,2,128]{3,1,2,0:T(8,128)(2,1)} async-done(((bf16[1,256,2,128]{3,1,2,0:T(8,128)(2,1)}), bf16[8,256,2,128]{3,1,2,0:T(8,128)(2,1)}) %all-gather.2.cloned.1.call-update) | async-done | bytes 1048592 | tf_op jit(solution)/shard_map/all_gather | solution.py:80
  56.7 1.4 fusion.104
  58.0 1.3 collective-permute-start.2
  59.4 1.3 collective-permute-start.3
  60.7 0.9 fusion.86
  61.6 1.0 fusion.78
  64.6 0.9 convolution_bitcast_fusion.1
  65.5 0.9 convolution_bitcast_fusion.2
  66.5 0.9 convolution_bitcast_fusion
  67.4 3.3 %fusion.54 = f32[8,64,2,128]{3,1,2,0:T(8,128)} fusion(f32[9,10,64,2,128]{4,2,3,1,0:T(8,128)S(1)} %convolution_bitcast_fusion, f32[9,10,64,2,128]{4,2,3,1,0:T(8,128)S(1)} %convolution_bitcast_fusion.1, f32[9,10,64,2,128]{4,2,0,3,1:T(8,128)S(1)} %convolution_bitcast_fusion.2), kind=kLoop, calls=%fused_computation.90 | loop fusion | flops 3407872 | bytes 22937600 | tf_op jit(solution)/shard_map/add | solution.py:98
  70.8 2.5 %convolution_bitcast_fusion.3 = f32[9,256,64]{1,2,0:T(8,128)S(1)} fusion(bf16[8,9,64,2,128]{4,2,3,0,1:T(8,128)(2,1)} %fusion.68, bf16[8,256,2,128]{3,1,2,0:T(8,128)(2,1)S(1)} %copy-done), kind=kOutput, calls=%fused_computation.55 | convolution fusion | flops 603979776 | bytes 3997696 | tf_op jit(solution)/shard_map/hodw,htcdw->toc/dot_general | solution.py:60
  73.3 2.5 %convolution_bitcast_fusion.4 = f32[9,256,64]{1,2,0:T(8,128)S(1)} fusion(bf16[8,9,64,2,128]{4,2,3,0,1:T(8,128)(2,1)} %get-tuple-element.9, bf16[8,256,2,128]{3,1,2,0:T(8,128)(2,1)S(1)} %copy-done), kind=kOutput, calls=%fused_computation.56 | convolution fusion | flops 603979776 | bytes 3997696 | tf_op jit(solution)/shard_map/hodw,htcdw->toc/dot_general | solution.py:60
  75.8 2.6 %fusion.19 = f32[9,256,64]{1,2,0:T(8,128)S(1)} fusion(bf16[8,9,64,2,128]{4,2,1,3,0:T(8,128)(2,1)} %fusion.86, bf16[8,256,2,128]{3,1,2,0:T(8,128)(2,1)S(1)} %copy-done), kind=kOutput, calls=%fused_computation.54 | convolution fusion | flops 603979776 | bytes 3997696 | tf_op jit(solution)/shard_map/hodw,htcdw->toc/dot_general | solution.py:60
  78.3 1.4 pad_maximum_fusion
  80.0 2.7 %fusion.13 = f32[8,2,128,256,1]{3,2,0,1,4:T(8,128)S(1)} fusion(bf16[8,9,64,2,128]{4,2,3,0,1:T(8,128)(2,1)} %get-tuple-element.9, bf16[27,256,64]{1,2,0:T(8,128)(2,1)S(1)} %copy-done.1), kind=kOutput, calls=%fused_computation.40 | convolution fusion | flops 603979776 | bytes 4751360 | tf_op jit(solution)/shard_map/toc,htcdw->hodw/dot_general | solution.py:35
  82.7 2.7 %fusion.11 = f32[8,2,128,256,1]{3,2,0,1,4:T(8,128)S(1)} fusion(bf16[8,9,64,2,128]{4,2,3,0,1:T(8,128)(2,1)} %fusion.68, bf16[27,256,64]{1,2,0:T(8,128)(2,1)S(1)} %copy-done.1), kind=kOutput, calls=%fused_computation.38 | convolution fusion | flops 603979776 | bytes 4751360 | tf_op jit(solution)/shard_map/toc,htcdw->hodw/dot_general | solution.py:35
  85.5 4.1 %fusion.15 = f32[8,256,2,128]{1,3,2,0:T(8,128)} fusion(f32[8,2,128,256,1]{3,2,0,1,4:T(8,128)S(1)} %fusion.11, f32[8,2,128,256,1]{3,2,0,1,4:T(8,128)S(1)} %fusion.13, bf16[8,9,64,2,128]{4,2,1,3,0:T(8,128)(2,1)} %fusion.86, bf16[27,256,64]{1,2,0:T(8,128)(2,1)S(1)} %copy-done.1), kind=kOutput, calls=%fused_computation.43 | convolution fusion | flops 605028352 | bytes 8945664 | tf_op jit(solution)/shard_map/toc,htcdw->hodw/dot_general | solution.py:35
  89.6 1.0 convert_element_type.15
  91.4 17.4 %all-reduce.7.cloned.1.call-done = f32[27,256,64]{1,2,0:T(8,128)} async-done(((f32[27,256,64]{1,2,0:T(8,128)}), f32[27,256,64]{1,2,0:T(8,128)}) %all-reduce.7.cloned.1.call-update) | async-done | bytes 1769488 | tf_op jit(solution)/shard_map/psum | solution.py:112
  108.8 2.9 %broadcast_multiply_fusion = f32[27,256,64]{1,2,0:T(8,128)} fusion(f32[27,256,64]{1,2,0:T(8,128)} %all-reduce.7.cloned.1.call-done), kind=kLoop, calls=%fused_computation.58 | loop fusion | flops 442368 | bytes 3538944 | tf_op jit(solution)/shard_map/mul | solution.py:114
  111.7 69.4 %reduce-scatter.3.cloned.1.call-done = f32[1,256,2,128]{1,3,2,0:T(8,128)} async-done(((f32[8,256,2,128]{1,3,2,0:T(8,128)}), f32[1,256,2,128]{1,3,2,0:T(8,128)}) %reduce-scatter.3.cloned.1.call-update) | async-done | bytes 262160 | tf_op jit(solution)/shard_map/reduce_scatter | solution.py:74
  181.1 1.0 convert_element_type.14
  (36 shorter events, 13.6 us)
Async XLA Ops:
  7.2 49.5 %all-gather.2.cloned.1.call-start = ((), (), s32[]{:S(2)}) async-start(), calls=%async_computation.3 | async-start | bytes 1179648 | tf_op jit(solution)/shard_map/all_gather | solution.py:80
  8.2 5.3 %collective-permute-start = (bf16[8,64,1,128]{3,1,2,0:T(8,128)(2,1)S(1)}, bf16[8,64,1,128]{3,1,2,0:T(8,128)(2,1)S(1)}, u32[]{:S(2)}, u32[]{:S(2)}) collective-permute-start(bf16[8,64,1,128]{3,1,2,0:T(8,128)(2,1)S(1)} %get-tuple-element.25), channel_id=1, source_target_pairs={{0,1},{2,3},{4,5},{6,7},{8,9},{10,11},{12,13},{14,15},{16,17},{18,... | collective-permute-start | bytes 393224 | tf_op jit(solution)/shard_map/ppermute | solution.py:15
  10.6 3.2 %collective-permute-start.1 = (bf16[8,64,1,128]{3,1,2,0:T(8,128)(2,1)S(1)}, bf16[8,64,1,128]{3,1,2,0:T(8,128)(2,1)S(1)}, u32[]{:S(2)}, u32[]{:S(2)}) collective-permute-start(bf16[8,64,1,128]{3,1,2,0:T(8,128)(2,1)S(1)} %get-tuple-element.26), channel_id=1, source_target_pairs={{1,0},{3,2},{5,4},{7,6},{9,8},{11,10},{13,12},{15,14},{17,16},{19,... | collective-permute-start | bytes 393224 | tf_op jit(solution)/shard_map/ppermute | solution.py:16
  13.5 76.1 %reduce-scatter.5.cloned.1.call-start = ((), (), s32[]{:S(2)}) async-start(), calls=%async_computation.4 | async-start | bytes 786432 | tf_op jit(solution)/shard_map/reduce_scatter | solution.py:107
  16.8 5.2 %copy-start.2 = (bf16[8,64,2,128]{3,2,1,0:T(2,128)(2,1)S(1)}, bf16[8,64,2,128]{3,2,1,0:T(2,128)(2,1)}, u32[]{:S(2)}) copy-start(bf16[8,64,2,128]{3,2,1,0:T(2,128)(2,1)} %param.3) | copy-start | bytes 786436
  56.7 6.8 %copy-start = (bf16[8,256,2,128]{3,1,2,0:T(8,128)(2,1)S(1)}, bf16[8,256,2,128]{3,1,2,0:T(8,128)(2,1)}, u32[]{:S(2)}) copy-start(bf16[8,256,2,128]{3,1,2,0:T(8,128)(2,1)} %all-gather.2.cloned.1.call-done) | copy-start | bytes 3145732
  58.0 5.4 %collective-permute-start.2 = (bf16[8,256,1,128]{3,1,2,0:T(8,128)(2,1)S(1)}, bf16[8,256,1,128]{3,1,2,0:T(8,128)(2,1)S(1)}, u32[]{:S(2)}, u32[]{:S(2)}) collective-permute-start(bf16[8,256,1,128]{3,1,2,0:T(8,128)(2,1)S(1)} %get-tuple-element.23), channel_id=1, source_target_pairs={{0,1},{2,3},{4,5},{6,7},{8,9},{10,11},{12,13},{14,15},{16,17},{18,... | collective-permute-start | bytes 1572872 | tf_op jit(solution)/shard_map/ppermute | solution.py:15
  59.4 4.1 %collective-permute-start.3 = (bf16[8,256,1,128]{3,1,2,0:T(8,128)(2,1)S(1)}, bf16[8,256,1,128]{3,1,2,0:T(8,128)(2,1)S(1)}, u32[]{:S(2)}, u32[]{:S(2)}) collective-permute-start(bf16[8,256,1,128]{3,1,2,0:T(8,128)(2,1)S(1)} %get-tuple-element.24), channel_id=1, source_target_pairs={{1,0},{3,2},{5,4},{7,6},{9,8},{11,10},{13,12},{15,14},{17,16},{19,... | collective-permute-start | bytes 1572872 | tf_op jit(solution)/shard_map/ppermute | solution.py:16
  63.4 1.2 copy-start.1
  70.8 38.1 %all-reduce.7.cloned.1.call-start = ((), (), s32[]{:S(2)}) async-start(), calls=%async_computation.5 | async-start | bytes 3538944 | tf_op jit(solution)/shard_map/psum | solution.py:112
  79.7 101.4 %reduce-scatter.3.cloned.1.call-start = ((), (), s32[]{:S(2)}) async-start(), calls=%async_computation.2 | async-start | bytes 2359296 | tf_op jit(solution)/shard_map/reduce_scatter | solution.py:74
Sparse Core Ops, SparseCore 0:
  13.6 42.9 all-gather.1
  70.9 14.0 reduce-scatter.4
  88.1 20.6 all-reduce.6
  112.2 68.8 reduce-scatter.2
where the time goes:
time: 190 us; the launch traced here: 189 us
  waiting for transfers between devices  115 us (61%)
  local copies, waits for them, and re-layouts  21.9 us (12%)
  matrix products  19.9 us (10%)
  between operations  13.9 us (7%)
  other arithmetic  11.9 us (6%)
  starting transfers between devices  6.61 us (3%)
    reduce_scatter x1, waiting for transfers between devices, per_device(): lax.psum_scatter(conv_rows(block, kernel, lax.axis_size('cin') * rows_own...  69.4 us
    all_gather x1, waiting for transfers between devices, per_device(): grad_full = lax.all_gather(grad_out, 'cin', axis=0, tiled=True)  28 us
    unnamed x25, local copies, waits for them, and re-layouts  17.7 us
    psum x1, waiting for transfers between devices, per_device(): summed = lax.psum(local_terms, 'depth')  17.4 us
    dot_general x3, matrix products, conv_rows(): jnp.einsum('toc,htcdw->hodw', weight[9 * depth_off:9 * depth_off + 9], st...  9.56 us
    dot_general x3, matrix products, weight_terms(): jnp.einsum('hodw,htcdw->toc', grad_own, stacked, preferred_element_type=j...  7.5 us
  transfers between devices with their start and end apart: 8, of which 4 were waited for; matrix products, arithmetic and copies ran while one was open for 22% of the time, Pallas kernels for 0%

commit v1 on v0

--- a/solution.py
+++ b/solution.py
@@ -77,7 +77,27 @@
         scatter_dimension=0,
         tiled=True,
     ).astype(jnp.bfloat16)
-    grad_full = lax.all_gather(grad_out, "cin", axis=0, tiled=True)
+    w1 = lax.axis_size("cin")
+    v_now = lax.axis_index("cin")
+    e_next, step_out, outer = (w1, v_now, grad_out.shape[0])
+    in_order = [(h, (h + 1) % e_next) for h in range(e_next)]
+    entries = [(h, (h - 1) % e_next) for h in range(e_next)]
+    grad_full = jnp.zeros(
+        (*grad_out.shape[:0], e_next * outer, *grad_out.shape[1:]), grad_out.dtype
+    )
+    grad_full = lax.dynamic_update_slice_in_dim(grad_full, grad_out, step_out * outer, axis=0)
+    arr_out = k_now = grad_out
+    prior = e_next // 2
+    for no in range(1, prior + 1):
+        arr_out = lax.ppermute(arr_out, "cin", perm=in_order)
+        grad_full = lax.dynamic_update_slice_in_dim(
+            grad_full, arr_out, (step_out - no) % e_next * outer, axis=0
+        )
+        if no < e_next - prior:
+            k_now = lax.ppermute(k_now, "cin", perm=entries)
+            grad_full = lax.dynamic_update_slice_in_dim(
+                grad_full, k_now, (step_out + no) % e_next * outer, axis=0
+            )
     grad_full = padded_2(grad_full, (("depth", 2),), 1)
     grad_pad = jnp.pad(grad_full, ((1, 1), (0, 0), (0, 0), (0, 0)))
     rows_grad = rows_all // lax.axis_size("cout")

time: 190 us -> 155 us (0.82)
  waiting for transfers between devices: 115 us -> 79.4 us
  starting transfers between devices: 6.61 us -> 22.2 us
  matrix products: 19.9 us -> 11.4 us
  local copies, waits for them, and re-layouts: 21.9 us -> 14.6 us
  between operations: 13.9 us -> 16 us
    all_gather x1 -> x0, waiting for transfers between devices: 28 us -> none  [per_device(): grad_full = lax.all_gather(grad_out, 'cin', axis=0, tiled=True)]
    ppermute x0 -> x7, starting transfers between devices: none -> 15.6 us  [the longest x3 9.39 us: per_device(): k_now = lax.ppermute(k_now, 'cin', perm=entries)]
    reduce_scatter x1, waiting for transfers between devices: 69.4 us -> 56.2 us  [per_device(): lax.psum_scatter(conv_rows(block, kernel, lax.axis_size('cin') * rows_own...]
    ppermute x0 -> x7, waiting for transfers between devices: none -> 12.6 us  [the longest x4 12.3 us: per_device(): arr_out = lax.ppermute(arr_out, 'cin', perm=in_order)]
    psum x1, waiting for transfers between devices: 17.4 us -> 10.4 us  [per_device(): summed = lax.psum(local_terms, 'depth')]
    unnamed x25 -> x43, local copies, waits for them, and re-layouts: 17.7 us -> 11.6 us
    dot_general x3, matrix products: 9.56 us -> 4.54 us  [conv_rows(): jnp.einsum('toc,htcdw->hodw', weight[9 * depth_off:9 * depth_off + 9], st...]
    dot_general x3, matrix products: 7.5 us -> 4.08 us  [weight_terms(): jnp.einsum('hodw,htcdw->toc', grad_own, stacked, preferred_element_type=j...]
  transfers between devices with their start and end apart: 8 -> 14, of which waited for: 4 -> 8; matrix products, arithmetic and copies ran while one was open for 22% -> 15% of each run, Pallas kernels for 0% -> 0%
where the time goes in v1:
time: 155 us; the launch traced here: 154 us
  waiting for transfers between devices  79.4 us (51%)
  starting transfers between devices  22.2 us (14%)
  between operations  16 us (10%)
  local copies, waits for them, and re-layouts  14.6 us (9%)
  matrix products  11.4 us (7%)
  other arithmetic  10.4 us (7%)
    reduce_scatter x1, waiting for transfers between devices, per_device(): lax.psum_scatter(conv_rows(block, kernel, lax.axis_size('cin') * rows_own...  56.2 us
    ppermute x4, waiting for transfers between devices, per_device(): arr_out = lax.ppermute(arr_out, 'cin', perm=in_order)  12.3 us
    unnamed x43, local copies, waits for them, and re-layouts  11.6 us
    psum x1, waiting for transfers between devices, per_device(): summed = lax.psum(local_terms, 'depth')  10.4 us
    ppermute x3, starting transfers between devices, per_device(): k_now = lax.ppermute(k_now, 'cin', perm=entries)  9.39 us
    ppermute x4, starting transfers between devices, per_device(): arr_out = lax.ppermute(arr_out, 'cin', perm=in_order)  6.24 us
    dot_general x3, matrix products, conv_rows(): jnp.einsum('toc,htcdw->hodw', weight[9 * depth_off:9 * depth_off + 9], st...  4.54 us
    dot_general x3, matrix products, weight_terms(): jnp.einsum('hodw,htcdw->toc', grad_own, stacked, preferred_element_type=j...  4.08 us
  transfers between devices with their start and end apart: 14, of which 8 were waited for; matrix products, arithmetic and copies ran while one was open for 15% of the time, Pallas kernels for 0%

profile of v1, /device:TPU:0, one launch (start us, length us, event | category | flops | bytes accessed | tf_op | source)
XLA Modules:
  0.0 154.0 jit_solution(16493737149580959628)
XLA Ops:
  8.0 1.0 copy.6
  9.1 2.4 %collective-permute-start = (bf16[8,64,1,128]{3,1,2,0:T(8,128)(2,1)S(1)}, bf16[8,64,1,128]{3,1,2,0:T(8,128)(2,1)S(1)}, u32[]{:S(2)}, u32[]{:S(2)}) collective-permute-start(bf16[8,64,1,128]{3,1,2,0:T(8,128)(2,1)S(1)} %get-tuple-element.22), channel_id=1, source_target_pairs={{0,1},{2,3},{4,5},{6,7},{8,9},{10,11},{12,13},{14,15},{16,17},{18,... | collective-permute-start | bytes 393224 | tf_op jit(solution)/shard_map/ppermute | solution.py:15
  11.5 1.3 collective-permute-start.1
  13.0 1.6 %fusion.106 = (bf16[1,256,2,128]{3,1,2,0:T(8,128)(2,1)}, bf16[8,256,2,128]{3,1,2,0:T(8,128)(2,1)S(1)}) fusion(bf16[1,256,2,128]{3,2,1,0:T(2,128)(2,1)} %param.5, bf16[8,256,2,128]{3,1,2,0:T(8,128)(2,1)S(1)} %broadcast_in_dim.3, s32[]{:T(128)S(6)} %select_n.55), kind=kLoop, calls=%fused_computation.183 | loop fusion | bytes 393220 | tf_op args[2]
  14.6 2.3 %collective-permute-start.2 = (bf16[1,256,2,128]{3,1,2,0:T(8,128)(2,1)}, bf16[1,256,2,128]{3,1,2,0:T(8,128)(2,1)}, u32[]{:S(2)}, u32[]{:S(2)}) collective-permute-start(bf16[1,256,2,128]{3,1,2,0:T(8,128)(2,1)} %get-tuple-element.24), channel_id=1, source_target_pairs={{0,4},{4,8},{8,12},{12,16},{16,20},{20,24},{24,28},{28,0},{1,5},{5... | collective-permute-start | bytes 393224 | tf_op jit(solution)/shard_map/ppermute | solution.py:92
  16.9 3.0 %collective-permute-start.3 = (bf16[1,256,2,128]{3,1,2,0:T(8,128)(2,1)}, bf16[1,256,2,128]{3,1,2,0:T(8,128)(2,1)}, u32[]{:S(2)}, u32[]{:S(2)}) collective-permute-start(bf16[1,256,2,128]{3,1,2,0:T(8,128)(2,1)} %get-tuple-element.24), channel_id=1, source_target_pairs={{0,28},{4,0},{8,4},{12,8},{16,12},{20,16},{24,20},{28,24},{1,29},{... | collective-permute-start | bytes 393224 | tf_op jit(solution)/shard_map/ppermute | solution.py:97
  24.4 1.9 %collective-permute-start.4 = (bf16[1,256,2,128]{3,1,2,0:T(8,128)(2,1)}, bf16[1,256,2,128]{3,1,2,0:T(8,128)(2,1)S(1)}, u32[]{:S(2)}, u32[]{:S(2)}) collective-permute-start(bf16[1,256,2,128]{3,1,2,0:T(8,128)(2,1)} %collective-permute-done.2), channel_id=1, source_target_pairs={{0,4},{4,8},{8,12},{12,16},{16,20},{20,24},{24,28},{28,0},{1,5},{5... | collective-permute-start | bytes 393224 | tf_op jit(solution)/shard_map/ppermute | solution.py:92
  26.5 2.9 %collective-permute-start.5 = (bf16[1,256,2,128]{3,1,2,0:T(8,128)(2,1)}, bf16[1,256,2,128]{3,1,2,0:T(8,128)(2,1)S(1)}, u32[]{:S(2)}, u32[]{:S(2)}) collective-permute-start(bf16[1,256,2,128]{3,1,2,0:T(8,128)(2,1)} %collective-permute-done.3), channel_id=1, source_target_pairs={{0,28},{4,0},{8,4},{12,8},{16,12},{20,16},{24,20},{28,24},{1,29},{... | collective-permute-start | bytes 393224 | tf_op jit(solution)/shard_map/ppermute | solution.py:97
  30.3 0.9 constant_dynamic-update-slice_fusion.5
  31.2 2.3 %collective-permute-done.4 = bf16[1,256,2,128]{3,1,2,0:T(8,128)(2,1)S(1)} collective-permute-done((bf16[1,256,2,128]{3,1,2,0:T(8,128)(2,1)}, bf16[1,256,2,128]{3,1,2,0:T(8,128)(2,1)S(1)}, u32[]{:S(2)}, u32[]{:S(2)}) %collective-permute-start.4) | collective-permute-done | bytes 131104 | tf_op jit(solution)/shard_map/ppermute | solution.py:92
  33.5 1.3 collective-permute-start.6
  34.8 3.5 %collective-permute-start.7 = (bf16[1,256,2,128]{3,1,2,0:T(8,128)(2,1)S(1)}, bf16[1,256,2,128]{3,1,2,0:T(8,128)(2,1)S(1)}, u32[]{:S(2)}, u32[]{:S(2)}) collective-permute-start(bf16[1,256,2,128]{3,1,2,0:T(8,128)(2,1)S(1)} %collective-permute-done.5), channel_id=1, source_target_pairs={{0,28},{4,0},{8,4},{12,8},{16,12},{20,16},{24,20},{28,24},{1,29},{... | collective-permute-start | bytes 393224 | tf_op jit(solution)/shard_map/ppermute | solution.py:97
  38.3 3.2 %collective-permute-done.6 = bf16[1,256,2,128]{3,1,2,0:T(8,128)(2,1)S(1)} collective-permute-done((bf16[1,256,2,128]{3,1,2,0:T(8,128)(2,1)S(1)}, bf16[1,256,2,128]{3,1,2,0:T(8,128)(2,1)S(1)}, u32[]{:S(2)}, u32[]{:S(2)}) %collective-permute-start.6) | collective-permute-done | bytes 131104 | tf_op jit(solution)/shard_map/ppermute | solution.py:92
  42.6 6.6 %collective-permute-done.8 = bf16[1,256,2,128]{3,1,2,0:T(8,128)(2,1)S(1)} collective-permute-done((bf16[1,256,2,128]{3,1,2,0:T(8,128)(2,1)S(1)}, bf16[1,256,2,128]{3,1,2,0:T(8,128)(2,1)S(1)}, u32[]{:S(2)}, u32[]{:S(2)}) %collective-permute-start.8) | collective-permute-done | bytes 131104 | tf_op jit(solution)/shard_map/ppermute | solution.py:92
  49.3 1.3 collective-permute-start.9
  50.6 1.3 collective-permute-start.10
  52.7 1.5 %copy-done = bf16[8,9,64,2,128]{4,2,3,0,1:T(8,128)(2,1)} copy-done((bf16[8,9,64,2,128]{4,2,3,0,1:T(8,128)(2,1)}, bf16[8,9,64,2,128]{4,2,3,0,1:T(8,128)(2,1)S(1)}, u32[]{:S(2)}) %copy-start) | copy-done | bytes 2359320
  54.8 0.9 convolution_bitcast_fusion.1
  55.7 0.9 convolution_bitcast_fusion.2
  56.7 0.9 convolution_bitcast_fusion
  57.6 3.3 %fusion.54 = f32[8,64,2,128]{3,1,2,0:T(8,128)} fusion(f32[9,10,64,2,128]{4,2,3,1,0:T(8,128)S(1)} %convolution_bitcast_fusion, f32[9,10,64,2,128]{4,2,3,1,0:T(8,128)S(1)} %convolution_bitcast_fusion.1, f32[9,10,64,2,128]{4,2,0,3,1:T(8,128)S(1)} %convolution_bitcast_fusion.2), kind=kLoop, calls=%fused_computation.90 | loop fusion | flops 3407872 | bytes 22937600 | tf_op jit(solution)/shard_map/add | solution.py:118
  61.1 2.5 %convolution_bitcast_fusion.3 = f32[9,256,64]{1,2,0:T(8,128)S(1)} fusion(bf16[8,9,64,2,128]{4,2,3,0,1:T(8,128)(2,1)} %copy-done, bf16[8,256,2,128]{3,1,2,0:T(8,128)(2,1)S(1)} %constant_dynamic-update-slice_fusion), kind=kOutput, calls=%fused_computation.55 | convolution fusion | flops 603979776 | bytes 3997696 | tf_op jit(solution)/shard_map/hodw,htcdw->toc/dot_general | solution.py:60
  64.4 1.0 copy-done.3
  66.3 1.4 pad_maximum_fusion
  67.8 1.0 fusion.13
  69.4 1.0 fusion.11
  71.1 2.5 %fusion.15 = f32[8,256,2,128]{1,3,2,0:T(8,128)} fusion(f32[8,2,128,256,1]{3,2,0,1,4:T(8,128)S(1)} %fusion.11, f32[8,2,128,256,1]{3,2,0,1,4:T(8,128)S(1)} %fusion.13, bf16[8,9,64,2,128]{4,2,1,3,0:T(8,128)(2,1)S(1)} %copy-done.4, bf16[27,256,64]{1,2,0:T(8,128)(2,1)S(1)} %copy-done.8), kind=kOutput, calls=%fused_computation.43 | convolution fusion | flops 605028352 | bytes 8945664 | tf_op jit(solution)/shard_map/toc,htcdw->hodw/dot_general | solution.py:35
  73.6 1.0 convert_element_type.15
  75.4 10.4 %all-reduce.7.cloned.1.call-done = f32[27,256,64]{1,2,0:T(8,128)} async-done(((f32[27,256,64]{1,2,0:T(8,128)}), f32[27,256,64]{1,2,0:T(8,128)}) %all-reduce.7.cloned.1.call-update) | async-done | bytes 1769488 | tf_op jit(solution)/shard_map/psum | solution.py:132
  85.8 2.9 %broadcast_multiply_fusion = f32[27,256,64]{1,2,0:T(8,128)} fusion(f32[27,256,64]{1,2,0:T(8,128)} %all-reduce.7.cloned.1.call-done), kind=kLoop, calls=%fused_computation.58 | loop fusion | flops 442368 | bytes 3538944 | tf_op jit(solution)/shard_map/mul | solution.py:134
  88.6 56.2 %reduce-scatter.3.cloned.1.call-done = f32[1,256,2,128]{1,3,2,0:T(8,128)} async-done(((f32[8,256,2,128]{1,3,2,0:T(8,128)}), f32[1,256,2,128]{1,3,2,0:T(8,128)}) %reduce-scatter.3.cloned.1.call-update) | async-done | bytes 262160 | tf_op jit(solution)/shard_map/reduce_scatter | solution.py:74
  144.8 1.0 convert_element_type.14
  (73 shorter events, 12.8 us)
Async XLA Ops:
  8.0 65.6 %reduce-scatter.5.cloned.1.call-start = ((), (), s32[]{:S(2)}) async-start(), calls=%async_computation.3 | async-start | bytes 786432 | tf_op jit(solution)/shard_map/reduce_scatter | solution.py:127
  9.0 10.9 %copy-start.5 = (bf16[8,64,2,128]{3,1,2,0:T(8,128)(2,1)}, bf16[8,64,2,128]{3,1,2,0:T(8,128)(2,1)S(1)}, u32[]{:S(2)}) copy-start(bf16[8,64,2,128]{3,1,2,0:T(8,128)(2,1)S(1)} %copy.6) | copy-start | bytes 786436
  9.1 10.9 %collective-permute-start = (bf16[8,64,1,128]{3,1,2,0:T(8,128)(2,1)S(1)}, bf16[8,64,1,128]{3,1,2,0:T(8,128)(2,1)S(1)}, u32[]{:S(2)}, u32[]{:S(2)}) collective-permute-start(bf16[8,64,1,128]{3,1,2,0:T(8,128)(2,1)S(1)} %get-tuple-element.22), channel_id=1, source_target_pairs={{0,1},{2,3},{4,5},{6,7},{8,9},{10,11},{12,13},{14,15},{16,17},{18,... | collective-permute-start | bytes 393224 | tf_op jit(solution)/shard_map/ppermute | solution.py:15
  11.5 8.5 %collective-permute-start.1 = (bf16[8,64,1,128]{3,1,2,0:T(8,128)(2,1)S(1)}, bf16[8,64,1,128]{3,1,2,0:T(8,128)(2,1)S(1)}, u32[]{:S(2)}, u32[]{:S(2)}) collective-permute-start(bf16[8,64,1,128]{3,1,2,0:T(8,128)(2,1)S(1)} %get-tuple-element.23), channel_id=1, source_target_pairs={{1,0},{3,2},{5,4},{7,6},{9,8},{11,10},{13,12},{15,14},{17,16},{19,... | collective-permute-start | bytes 393224 | tf_op jit(solution)/shard_map/ppermute | solution.py:16
  14.6 9.8 %collective-permute-start.2 = (bf16[1,256,2,128]{3,1,2,0:T(8,128)(2,1)}, bf16[1,256,2,128]{3,1,2,0:T(8,128)(2,1)}, u32[]{:S(2)}, u32[]{:S(2)}) collective-permute-start(bf16[1,256,2,128]{3,1,2,0:T(8,128)(2,1)} %get-tuple-element.24), channel_id=1, source_target_pairs={{0,4},{4,8},{8,12},{12,16},{16,20},{20,24},{24,28},{28,0},{1,5},{5... | collective-permute-start | bytes 393224 | tf_op jit(solution)/shard_map/ppermute | solution.py:92
  16.9 9.5 %collective-permute-start.3 = (bf16[1,256,2,128]{3,1,2,0:T(8,128)(2,1)}, bf16[1,256,2,128]{3,1,2,0:T(8,128)(2,1)}, u32[]{:S(2)}, u32[]{:S(2)}) collective-permute-start(bf16[1,256,2,128]{3,1,2,0:T(8,128)(2,1)} %get-tuple-element.24), channel_id=1, source_target_pairs={{0,28},{4,0},{8,4},{12,8},{16,12},{20,16},{24,20},{28,24},{1,29},{... | collective-permute-start | bytes 393224 | tf_op jit(solution)/shard_map/ppermute | solution.py:97
  20.0 0.7 copy-start.10
  21.1 1.0 copy-start.6
  21.2 1.0 copy-start.11
  21.7 1.5 %copy-start.9 = (bf16[8,64,2,128]{3,2,1,0:T(2,128)(2,1)S(1)}, bf16[8,64,2,128]{3,2,1,0:T(2,128)(2,1)}, u32[]{:S(2)}) copy-start(bf16[8,64,2,128]{3,2,1,0:T(2,128)(2,1)} %param.3) | copy-start | bytes 786436
  24.4 9.2 %collective-permute-start.4 = (bf16[1,256,2,128]{3,1,2,0:T(8,128)(2,1)}, bf16[1,256,2,128]{3,1,2,0:T(8,128)(2,1)S(1)}, u32[]{:S(2)}, u32[]{:S(2)}) collective-permute-start(bf16[1,256,2,128]{3,1,2,0:T(8,128)(2,1)} %collective-permute-done.2), channel_id=1, source_target_pairs={{0,4},{4,8},{8,12},{12,16},{16,20},{20,24},{24,28},{28,0},{1,5},{5... | collective-permute-start | bytes 393224 | tf_op jit(solution)/shard_map/ppermute | solution.py:92
  26.5 8.3 %collective-permute-start.5 = (bf16[1,256,2,128]{3,1,2,0:T(8,128)(2,1)}, bf16[1,256,2,128]{3,1,2,0:T(8,128)(2,1)S(1)}, u32[]{:S(2)}, u32[]{:S(2)}) collective-permute-start(bf16[1,256,2,128]{3,1,2,0:T(8,128)(2,1)} %collective-permute-done.3), channel_id=1, source_target_pairs={{0,28},{4,0},{8,4},{12,8},{16,12},{20,16},{24,20},{28,24},{1,29},{... | collective-permute-start | bytes 393224 | tf_op jit(solution)/shard_map/ppermute | solution.py:97
  33.5 8.0 %collective-permute-start.6 = (bf16[1,256,2,128]{3,1,2,0:T(8,128)(2,1)S(1)}, bf16[1,256,2,128]{3,1,2,0:T(8,128)(2,1)S(1)}, u32[]{:S(2)}, u32[]{:S(2)}) collective-permute-start(bf16[1,256,2,128]{3,1,2,0:T(8,128)(2,1)S(1)} %collective-permute-done.4), channel_id=1, source_target_pairs={{0,4},{4,8},{8,12},{12,16},{16,20},{20,24},{24,28},{28,0},{1,5},{5... | collective-permute-start | bytes 393224 | tf_op jit(solution)/shard_map/ppermute | solution.py:92
  34.8 7.8 %collective-permute-start.7 = (bf16[1,256,2,128]{3,1,2,0:T(8,128)(2,1)S(1)}, bf16[1,256,2,128]{3,1,2,0:T(8,128)(2,1)S(1)}, u32[]{:S(2)}, u32[]{:S(2)}) collective-permute-start(bf16[1,256,2,128]{3,1,2,0:T(8,128)(2,1)S(1)} %collective-permute-done.5), channel_id=1, source_target_pairs={{0,28},{4,0},{8,4},{12,8},{16,12},{20,16},{24,20},{28,24},{1,29},{... | collective-permute-start | bytes 393224 | tf_op jit(solution)/shard_map/ppermute | solution.py:97
  41.5 7.7 %collective-permute-start.8 = (bf16[1,256,2,128]{3,1,2,0:T(8,128)(2,1)S(1)}, bf16[1,256,2,128]{3,1,2,0:T(8,128)(2,1)S(1)}, u32[]{:S(2)}, u32[]{:S(2)}) collective-permute-start(bf16[1,256,2,128]{3,1,2,0:T(8,128)(2,1)S(1)} %collective-permute-done.6), channel_id=1, source_target_pairs={{0,4},{4,8},{8,12},{12,16},{16,20},{20,24},{24,28},{28,0},{1,5},{5... | collective-permute-start | bytes 393224 | tf_op jit(solution)/shard_map/ppermute | solution.py:92
  49.3 3.4 %collective-permute-start.9 = (bf16[8,256,1,128]{3,1,2,0:T(8,128)(2,1)S(1)}, bf16[8,256,1,128]{3,1,2,0:T(8,128)(2,1)S(1)}, u32[]{:S(2)}, u32[]{:S(2)}) collective-permute-start(bf16[8,256,1,128]{3,1,2,0:T(8,128)(2,1)S(1)} %get-tuple-element.20), channel_id=1, source_target_pairs={{0,1},{2,3},{4,5},{6,7},{8,9},{10,11},{12,13},{14,15},{16,17},{18,... | collective-permute-start | bytes 1572872 | tf_op jit(solution)/shard_map/ppermute | solution.py:15
  50.6 3.8 %collective-permute-start.10 = (bf16[8,256,1,128]{3,1,2,0:T(8,128)(2,1)S(1)}, bf16[8,256,1,128]{3,1,2,0:T(8,128)(2,1)S(1)}, u32[]{:S(2)}, u32[]{:S(2)}) collective-permute-start(bf16[8,256,1,128]{3,1,2,0:T(8,128)(2,1)S(1)} %get-tuple-element.21), channel_id=1, source_target_pairs={{1,0},{3,2},{5,4},{7,6},{9,8},{11,10},{13,12},{15,14},{17,16},{19,... | collective-permute-start | bytes 1572872 | tf_op jit(solution)/shard_map/ppermute | solution.py:16
  52.1 4.5 %copy-start.2 = (bf16[8,9,64,2,128]{4,2,1,3,0:T(8,128)(2,1)}, bf16[8,9,64,2,128]{4,2,1,3,0:T(8,128)(2,1)S(1)}, u32[]{:S(2)}) copy-start(bf16[8,9,64,2,128]{4,2,1,3,0:T(8,128)(2,1)S(1)} %fusion.86) | copy-start | bytes 7077892
  52.7 1.6 %copy-start = (bf16[8,9,64,2,128]{4,2,3,0,1:T(8,128)(2,1)}, bf16[8,9,64,2,128]{4,2,3,0,1:T(8,128)(2,1)S(1)}, u32[]{:S(2)}) copy-start(bf16[8,9,64,2,128]{4,2,3,0,1:T(8,128)(2,1)S(1)} %fusion.68) | copy-start | bytes 7077892
  52.7 2.1 %copy-start.7 = (bf16[27,256,64]{1,2,0:T(8,128)(2,1)S(1)}, bf16[27,256,64]{1,2,0:T(8,128)(2,1)}, u32[]{:S(2)}) copy-start(bf16[27,256,64]{1,2,0:T(8,128)(2,1)} %param.4) | copy-start | bytes 2654212
  60.9 24.9 %all-reduce.7.cloned.1.call-start = ((), (), s32[]{:S(2)}) async-start(), calls=%async_computation.4 | async-start | bytes 3538944 | tf_op jit(solution)/shard_map/psum | solution.py:132
  63.6 1.8 %copy-start.3 = (bf16[8,9,64,2,128]{4,2,1,3,0:T(8,128)(2,1)S(1)}, bf16[8,9,64,2,128]{4,2,1,3,0:T(8,128)(2,1)}, u32[]{:S(2)}) copy-start(bf16[8,9,64,2,128]{4,2,1,3,0:T(8,128)(2,1)} %copy-done.2) | copy-start | bytes 7077892
  66.3 1.5 copy-start.8
  67.7 77.2 %reduce-scatter.3.cloned.1.call-start = ((), (), s32[]{:S(2)}) async-start(), calls=%async_computation.2 | async-start | bytes 2359296 | tf_op jit(solution)/shard_map/reduce_scatter | solution.py:74
  67.8 1.7 %copy-start.1 = (bf16[8,9,64,2,128]{4,2,3,0,1:T(8,128)(2,1)S(1)}, bf16[8,9,64,2,128]{4,2,3,0,1:T(8,128)(2,1)}, u32[]{:S(2)}) copy-start(bf16[8,9,64,2,128]{4,2,3,0,1:T(8,128)(2,1)} %copy-done) | copy-start | bytes 7077892
  69.4 1.7 %copy-start.4 = (bf16[8,9,64,2,128]{4,2,1,3,0:T(8,128)(2,1)S(1)}, bf16[8,9,64,2,128]{4,2,1,3,0:T(8,128)(2,1)}, u32[]{:S(2)}) copy-start(bf16[8,9,64,2,128]{4,2,1,3,0:T(8,128)(2,1)} %copy-done.2) | copy-start | bytes 7077892
Sparse Core Ops, SparseCore 0:
  61.0 12.2 reduce-scatter.4
  77.3 67.5 reduce-scatter.2
Sparse Core Ops, SparseCore 1:
  67.8 17.9 all-reduce.6
